TPU v7x, 32 devices: a whole 2x2x4 slice. The times are simulated.
32 devices in a mesh: row: 8 (over z, x), col: 4 (over y, core).
Axes of the slice: x: 2, y: 2, z: 4, core: 2. Of those that a mesh axis runs over, the one named last changes fastest.
Arguments:
- inputs: bfloat16 [640, 12288], P('row', 'col'), may hold values from -6 to 6
- pre_act: bfloat16 [640, 24576], P('col', 'row'), may hold values from -6 to 6
- out_grad: bfloat16 [640, 12288], P('row', 'col'), may hold values from -6 to 6
- token_valid: int32 [640], P('row'), may hold values 0 or 1
- poison: int32 [8, 4], P('row', 'col'), may hold values 0 or 1
- w_up: bfloat16 [12288, 24576], P('col', 'row'), may hold values from -0.0546875 to 0.0546875
- w_down: bfloat16 [24576, 12288], P('row', 'col'), may hold values from -0.0390625 to 0.0390625
Outputs:
- input_grad: bfloat16 [640, 12288], P('row', 'col')
- grad_up: bfloat16 [12288, 24576], P('col', 'row')
- grad_down: bfloat16 [24576, 12288], P('row', 'col')
All inputs are finite; a program needn't handle non-finite values. No bound on the sum of `token_valid` or of `poison` on one device may be relied on, other than what follows from the above.
Results may differ from a plain program's by a relative error of at most 0.0051.
Values may be sent and summed in bfloat16 or wider, within the bound.
No kernel may reach another device: no remote copies, remote signals or barrier semaphores. Data moves between devices by JAX's collectives and lax.ppermute only.
A program may use at most 384 MiB of HBM per device.

v0:
```python
import math

import jax
import jax.numpy as jnp
from jax import lax
from jax.experimental import pallas as pl
from jax.experimental.pallas import tpu as pltpu
from jax.sharding import PartitionSpec as P

F32 = jnp.float32
BF16 = jnp.bfloat16
LAST = (((1,), (1,)), ((), ()))
FIRST = (((0,), (0,)), ((), ()))
FACTOR = math.sqrt(2.0 / math.pi)
TILE = 256
VMEM_LIMIT = 56 * 1024 * 1024


def swap(value, axis, bit):
    size = lax.axis_size(axis)
    return lax.ppermute(value, axis, [(i, i ^ bit) for i in range(size)])


def bits_of(size):
    return [1 << i for i in range(size.bit_length() - 1)]


def turned(index, size):
    return sum(((index // bit) % 2) * (size // 2 // bit) for bit in bits_of(size))


def call(kernel, grid, in_specs, out_specs, out_shape, moved):
    return pl.pallas_call(
        kernel,
        grid_spec=pltpu.PrefetchScalarGridSpec(
            num_scalar_prefetch=1,
            grid=grid,
            in_specs=in_specs,
            out_specs=out_specs,
        ),
        out_shape=out_shape,
        compiler_params=pltpu.CompilerParams(
            dimension_semantics=("arbitrary",), vmem_limit_bytes=VMEM_LIMIT
        ),
        cost_estimate=pl.CostEstimate(
            flops=1000, bytes_accessed=moved, transcendentals=0
        ),
    )


def whole_index(i, flags):
    return (0, 0)


def column_index(i, flags):
    return (0, i)


def aligned(start):
    return pl.multiple_of(start, 16)


def token_place(index, core, per_group):
    group, k = index // 2 // per_group, index // 2 % per_group
    return (2 * group + (index % 2 ^ core)) * per_group + k


def widest(width, limit):
    return max(tile for tile in range(128, limit + 1, 128) if width % tile == 0)


def gelu_all(pieces, offsets, flags, n_row, per_group, rows):
    width = pieces[0].shape[1]
    per_col = pieces[0].shape[0] // rows
    tokens = n_row * rows
    tile = widest(width, 256)

    def kernel(flags_ref, *refs):
        act_ref, slope_ref = refs[-2:]
        row, core, col = flags_ref[0], flags_ref[1], flags_ref[2]
        for ref, offset in zip(refs[:-2], offsets):
            for part in range(per_col):
                index = row ^ ((col ^ offset) * per_col + part)
                hval = ref[part * rows : (part + 1) * rows, :].astype(F32)
                tanh_part = jnp.tanh(FACTOR * (hval + 0.044715 * hval * hval * hval))
                place = token_place(index, core, per_group)
                act_ref[pl.ds(aligned(place * rows), rows), :] = (
                    0.5 * hval * (1.0 + tanh_part)
                ).astype(BF16)

                @pl.when(index % 2 == core)
                def _():
                    slope_ref[pl.ds(aligned((index // 2) * rows), rows), :] = 0.5 * (
                        1.0 + tanh_part
                    ) + 0.5 * hval * (1.0 - tanh_part * tanh_part) * FACTOR * (
                        1.0 + 3.0 * 0.044715 * hval * hval
                    )

    return call(
        kernel,
        (width // tile,),
        [pl.BlockSpec((piece.shape[0], tile), column_index) for piece in pieces],
        [
            pl.BlockSpec((tokens, tile), column_index),
            pl.BlockSpec((tokens // 2, tile), column_index),
        ],
        [
            jax.ShapeDtypeStruct((tokens, width), BF16),
            jax.ShapeDtypeStruct((tokens // 2, width), F32),
        ],
        24 * tokens * width,
    )(flags, *pieces)


def arrange(pieces, places, rows, flags):
    width = pieces[0].shape[1]
    tokens = sum(piece.shape[0] for piece in pieces)
    tile = widest(width, width // 2)

    def kernel(flags_ref, *refs):
        for ref, blocks in zip(refs, places):
            for k, place in enumerate(blocks):
                start = aligned(place(flags_ref[1]) * rows)
                refs[-1][pl.ds(start, rows), :] = ref[k * rows : (k + 1) * rows, :]

    return call(
        kernel,
        (width // tile,),
        [pl.BlockSpec((piece.shape[0], tile), column_index) for piece in pieces],
        pl.BlockSpec((tokens, tile), column_index),
        jax.ShapeDtypeStruct((tokens, width), BF16),
        6 * tokens * width,
    )(flags, *pieces)


def gram(value):
    return lax.dot_general(value, value, LAST, preferred_element_type=F32)


def after(value, *events):
    return lax.optimization_barrier((value, *events))[0]


def on_device(inputs, pre_act, out_grad, token_valid, poison, w_up, w_down):
    n_row = lax.axis_size("row")
    n_col = lax.axis_size("col")
    rows = inputs.shape[0]
    tokens = rows * n_row
    slots = n_row // 2
    row, col = lax.axis_index("row"), lax.axis_index("col")
    core = col % 2
    flags = jnp.stack([row, core, col]).astype(jnp.int32)
    row_bits, col_bits = bits_of(n_row), bits_of(n_col)

    def first_hops(own, x_own, near_first):
        blocks = {0: own}
        for bit in row_bits:
            source = x_own if bit == 1 else own
            if near_first and bit == row_bits[-1]:
                source = after(source, blocks[1], blocks[2])
            blocks[bit] = swap(source, "row", bit)
        return blocks

    def other_hops(blocks, events=(), late=()):
        near, blocks = blocks, dict(blocks)
        for bit in reversed(row_bits[1:]):
            for index in sorted(blocks):
                if index > 0 and index % (2 * bit) == 0:
                    blocks[index | bit] = swap(after(blocks[index], *events), "row", bit)
        for index in sorted(blocks):
            if index > 0 and index % 2 == 0:
                source = after(blocks[index], *(events if index in near else late))
                blocks[index | 1] = swap(source, "row", 1)
        return [blocks[index] for index in range(n_row)]

    groups = 2 if slots % 2 == 0 else 1
    per_group = slots // groups
    count = per_group * rows
    by_group = [range(2 * g * per_group, 2 * (g + 1) * per_group) for g in range(groups)]

    pieces, offsets = [pre_act], [0]
    for bit in reversed(col_bits):
        pieces = pieces + [swap(piece, "col", bit) for piece in pieces]
        offsets = offsets + [offset ^ bit for offset in offsets]

    own = out_grad * token_valid.astype(BF16)[:, None]
    masked = other_hops(first_hops(own, own, True))
    own = after(inputs, masked[-2])

    blocks, totals, received = [], [], []
    for group, indices in enumerate(by_group):
        if group == 1:
            act, slope = gelu_all(
                [after(pieces[0], *totals)] + pieces[1:],
                offsets,
                flags,
                n_row,
                per_group,
                rows,
            )
            masked[-1] = swap(after(masked[-2], act, masked[n_row // 2 + 1]), "row", 1)
            inputs_hops = first_hops(own, after(own, masked[-1]), False)
        base = 2 * group * per_group
        block = arrange(
            [masked[index] for index in indices],
            [
                [lambda core, i=index, b=base: token_place(i, core, per_group) - b]
                for index in indices
            ],
            rows,
            flags,
        )
        blocks.append(block)
        if group == 0:
            first, second = [], [masked[n_row // 2], pieces[1]]
        else:
            first = received
            second = [inputs_hops[bit] for bit in row_bits]
        partial = lax.dot_general(
            after(block, *first), w_down, LAST, preferred_element_type=F32
        )
        total = partial[:count]
        got = swap(after(partial[count:].astype(BF16), *second), "col", 1)
        for bit in col_bits[1:]:
            total = total + got.astype(F32)
            got = swap(total.astype(BF16), "col", bit)
        totals.append(total)
        received.append(got)
    masked_all = arrange(
        [after(blocks[0], total)] + blocks[1:],
        [
            [lambda core, p=p: p for p in range(2 * g * per_group, 2 * (g + 1) * per_group)]
            for g in range(groups)
        ],
        rows,
        flags,
    )
    masked_gram = gram(masked_all)
    inputs_blocks = other_hops(inputs_hops, [partial], [masked_gram])
    hidden_blocks = []
    for group, (total, got) in enumerate(zip(totals, received)):
        if hidden_blocks:
            events = [inputs_blocks[3], inputs_blocks[n_row // 2 + 1]]
            got = after(got, hidden_blocks[-1], masked_gram, *events)
        total = total + got.astype(F32)
        hidden = (total * slope[group * count : (group + 1) * count]).astype(BF16)
        hidden_blocks += [hidden, swap(hidden, "col", 1)]
    square_down = jnp.sum(masked_gram * gram(after(act, hidden)))

    def exchange_place(side, slot, swapped):
        return lambda core: (side ^ (core & swapped)) * slots + turned(slot, slots)

    hidden_all = arrange(
        hidden_blocks,
        [
            [exchange_place(side, g * per_group + k, 1) for k in range(per_group)]
            for g in range(groups)
            for side in range(2)
        ],
        rows,
        flags,
    )

    flag_value = poison[0, 0].astype(F32)
    keep_block = 1.0 - flag_value
    count_term = jnp.where(col == 0, jnp.sum(token_valid.astype(F32)), 0.0)

    model = w_up.shape[0]
    parts = 3 if model % (3 * TILE) == 0 else 1
    step = model // parts
    sums = []
    operand = hidden_all
    for part in range(parts):
        product = lax.dot_general(
            operand, w_up[part * step : (part + 1) * step], LAST, preferred_element_type=F32
        )
        theirs = product[tokens // 2 :].astype(BF16)
        sums.append((product[: tokens // 2], swap(theirs, "row", 1)))
        operand = after(operand, theirs, inputs_blocks[-1])

    inputs_all = arrange(
        [after(inputs_blocks[0], square_down, theirs)] + inputs_blocks[1:],
        [[exchange_place(index % 2, index // 2, 0)] for index in range(n_row)],
        rows,
        flags,
    )
    inputs_gram = gram(inputs_all)
    square_up = jnp.sum(inputs_gram * gram(hidden_all))
    scalars = jnp.stack([count_term, keep_block * (square_down + square_up), flag_value])
    for bit in col_bits:
        scalars = scalars + swap(scalars, "col", bit)
    for bit in row_bits[1:]:
        scalars = scalars + swap(scalars, "row", bit)
    stages = []
    for total, got in sums:
        stages.append([total + after(got, scalars).astype(F32)])
        for bit in row_bits[1:]:
            total = stages[-1][-1]
            split = total.shape[0] // 2
            got = swap(total[split:].astype(BF16), "row", bit)
            stages[-1].append(total[:split] + got.astype(F32))
    scalars = scalars + swap(scalars, "row", 1)
    count_all, square_all, flag_all = scalars[0], jnp.maximum(scalars[1], 0.0), scalars[2]

    token_total = jnp.maximum(count_all, 1.0)
    squares = square_all / (token_total * token_total)
    block_count = float(n_row * n_col)
    estimate = squares * block_count / jnp.maximum(block_count - flag_all, 1.0)
    limit = 0.25 * math.sqrt(
        (w_up.shape[1] * n_row) * (w_up.shape[0] * n_col) / tokens
    )
    clip_factor = jnp.minimum(1.0, limit / jnp.sqrt(estimate + 1e-06))
    scale = keep_block * clip_factor / token_total

    def gradient(left, right, scale):
        product = lax.dot_general(left, right, FIRST, preferred_element_type=F32)
        return (product * scale).astype(BF16)

    grad_down = gradient(act, masked_all, after(scale, *[stage[0] for stage in stages]))
    events = [stage[1] for stage in stages] + [grad_down]
    grad_up = gradient(inputs_all, hidden_all, after(scale, *events))
    input_sum = jnp.concatenate([stage[-1] for stage in stages], axis=1)
    return (input_sum / token_total).astype(BF16), grad_up, grad_down


def solution(mesh):
    placed = (
        P("row", "col"),
        P("col", "row"),
        P("row", "col"),
        P("row"),
        P("row", "col"),
        P("col", "row"),
        P("row", "col"),
    )
    return jax.shard_map(
        on_device,
        mesh=mesh,
        in_specs=placed,
        out_specs=(P("row", "col"), P("col", "row"), P("row", "col")),
        check_vma=False,
    )
```

profile of v0, /device:TPU:0, one launch (start us, length us, event | category | flops | bytes accessed | tf_op | source)
XLA Modules:
  0.0 253.9 jit_solution(7957003879711554056)
XLA Ops:
  2.4 3.1 %collective-permute-start.1 = (bf16[80,3072]{1,0:T(8,128)(2,1)S(1)}, bf16[80,3072]{1,0:T(8,128)(2,1)S(1)}, u32[]{:S(2)}, u32[]{:S(2)}) collective-permute-start(bf16[80,3072]{1,0:T(8,128)(2,1)S(1)} %broadcast_multiply_fusion.refs_0_), channel_id=1, source_target_pairs={{0,8},{4,12},{8,0},{12,4},{16,24},{20,28},{24,16},{28,20},{1,9},{5... | collective-permute-start | bytes 1474568 | tf_op jit(solution)/shard_map/ppermute | solution.py:21
  7.0 9.7 %collective-permute-done.1.refs_2_ = bf16[80,3072]{1,0:T(8,128)(2,1)S(1)} collective-permute-done((bf16[80,3072]{1,0:T(8,128)(2,1)S(1)}, bf16[80,3072]{1,0:T(8,128)(2,1)S(1)}, u32[]{:S(2)}, u32[]{:S(2)}) %collective-permute-start.1) | collective-permute-done | bytes 491552 | tf_op jit(solution)/shard_map/ppermute | solution.py:21
  23.2 6.0 %collective-permute-done.2.refs_3_ = bf16[80,3072]{1,0:T(8,128)(2,1)S(1)} collective-permute-done((bf16[80,3072]{1,0:T(8,128)(2,1)S(1)}, bf16[80,3072]{1,0:T(8,128)(2,1)S(1)}, u32[]{:S(2)}, u32[]{:S(2)}) %collective-permute-start.2) | collective-permute-done | bytes 491552 | tf_op jit(solution)/shard_map/ppermute | solution.py:21
  30.0 3.4 %shard_map.94.refs_0_ = bf16[320,3072]{1,0:T(8,128)(2,1)} custom-call(s32[3]{0:T(128)} %pad_add_fusion.flags_ref, bf16[80,3072]{1,0:T(8,128)(2,1)} %copy-done.7, bf16[80,3072]{1,0:T(8,128)(2,1)} %copy-done.17, bf16[80,3072]{1,0:T(8,128)(2,1)} %copy-done.16, bf16[80,3072]{1,0:T(8,128)(2,1)} %copy-done.18), custom_call_target="tpu_custom_call" | custom-call | flops 1000 | bytes 5898240 | tf_op jit(solution)/shard_map/pallas_call | solution.py:126
  33.4 10.8 %fusion.10 = f32[320,3072]{1,0:T(8,128)S(1)} fusion(bf16[320,3072]{1,0:T(8,128)(2,1)} %shard_map.94.refs_0_, bf16[3072,3072]{1,0:T(8,128)(2,1)} %param.13), kind=kOutput, calls=%fused_computation.43 | convolution fusion | flops 6039797760 | bytes 24772608 | tf_op jit(solution)/shard_map/dot_general | solution.py:219
  51.7 12.0 %shard_map.95 = (bf16[640,3072]{1,0:T(8,128)(2,1)}, f32[320,3072]{1,0:T(8,128)}) custom-call(s32[3]{0:T(128)} %pad_add_fusion.flags_ref, bf16[160,3072]{1,0:T(8,128)(2,1)} %refs_0_, bf16[160,3072]{1,0:T(8,128)(2,1)} %collective-permute-done.4.refs_1_, bf16[160,3072]{1,0:T(8,128)(2,1)} %copy-done.14, bf16[160,3072]{1,0:T(8,128)(2,1)} %copy-done.15), custom_call_target="tpu_custom_call" | custom-call | flops 1000 | bytes 47185920 | tf_op jit(solution)/shard_map/pallas_call | solution.py:99
  68.6 8.8 %collective-permute-done.12.refs_3_ = bf16[80,3072]{1,0:T(8,128)(2,1)S(1)} collective-permute-done((bf16[80,3072]{1,0:T(8,128)(2,1)}, bf16[80,3072]{1,0:T(8,128)(2,1)S(1)}, u32[]{:S(2)}, u32[]{:S(2)}) %collective-permute-start.12) | collective-permute-done | bytes 491552 | tf_op jit(solution)/shard_map/ppermute | solution.py:21
  78.1 3.4 %shard_map.96.refs_1_ = bf16[320,3072]{1,0:T(8,128)(2,1)} custom-call(s32[3]{0:T(128)} %pad_add_fusion.flags_ref, bf16[80,3072]{1,0:T(8,128)(2,1)} %collective-permute-done.3.refs_0_, bf16[80,3072]{1,0:T(8,128)(2,1)} %collective-permute-done.10.refs_1_, bf16[80,3072]{1,0:T(8,128)(2,1)} %collective-permute-done.11.refs_2_, bf16[80,3072]{1,0:T(8,128)(2,1)} %copy-done.20), custom_call_target="tpu_custom_call" | custom-call | flops 1000 | bytes 5898240 | tf_op jit(solution)/shard_map/pallas_call | solution.py:126
  81.5 10.9 %fusion.11 = f32[320,3072]{1,0:T(8,128)S(1)} fusion(bf16[320,3072]{1,0:T(8,128)(2,1)} %shard_map.96.refs_1_, bf16[3072,3072]{1,0:T(8,128)(2,1)} %param.13), kind=kOutput, calls=%fused_computation.44 | convolution fusion | flops 6039797760 | bytes 24772608 | tf_op jit(solution)/shard_map/dot_general | solution.py:219
  101.4 4.3 %shard_map.97 = bf16[640,3072]{1,0:T(8,128)(2,1)} custom-call(s32[3]{0:T(128)} %pad_add_fusion.flags_ref, bf16[320,3072]{1,0:T(8,128)(2,1)} %shard_map.94.refs_0_, bf16[320,3072]{1,0:T(8,128)(2,1)} %shard_map.96.refs_1_), custom_call_target="tpu_custom_call" | custom-call | flops 1000 | bytes 11796480 | tf_op jit(solution)/shard_map/pallas_call | solution.py:126
  105.7 7.7 %fusion.12 = f32[640,640]{1,0:T(8,128)} fusion(bf16[640,3072]{1,0:T(8,128)(2,1)} %shard_map.97), kind=kOutput, calls=%fused_computation.45 | convolution fusion | flops 2516582400 | bytes 5570560 | tf_op jit(solution)/shard_map/dot_general | solution.py:137
  113.4 9.5 %collective-permute-done.18.refs_3_ = bf16[80,3072]{1,0:T(8,128)(2,1)} collective-permute-done((bf16[80,3072]{1,0:T(8,128)(2,1)}, bf16[80,3072]{1,0:T(8,128)(2,1)}, u32[]{:S(2)}, u32[]{:S(2)}) %collective-permute-start.18) | collective-permute-done | bytes 491552 | tf_op jit(solution)/shard_map/ppermute | solution.py:21
  127.8 7.8 %multiply_reduce_fusion.1 = f32[]{:T(128)} fusion(f32[640,640]{1,0:T(8,128)} %fusion.12, bf16[640,3072]{1,0:T(8,128)(2,1)} %get-tuple-element.41), kind=kOutput, calls=%fused_computation.15 | convolution fusion | flops 2517401600 | bytes 5570564 | tf_op jit(solution)/shard_map/dot_general | solution.py:137
  136.5 4.2 %shard_map.98 = bf16[640,3072]{1,0:T(8,128)(2,1)} custom-call(s32[3]{0:T(128)} %pad_add_fusion.flags_ref, bf16[160,3072]{1,0:T(8,128)(2,1)} %copy-done.5, bf16[160,3072]{1,0:T(8,128)(2,1)} %copy-done.11, bf16[160,3072]{1,0:T(8,128)(2,1)} %copy-done.6, bf16[160,3072]{1,0:T(8,128)(2,1)} %copy-done.12), custom_call_target="tpu_custom_call" | custom-call | flops 1000 | bytes 11796480 | tf_op jit(solution)/shard_map/pallas_call | solution.py:126
  140.7 7.7 %fusion.4 = f32[640,1024]{1,0:T(8,128)S(1)} fusion(bf16[640,3072]{1,0:T(8,128)(2,1)} %shard_map.98, bf16[3072,3072]{1,0:T(8,128)(2,1)} %param.12), kind=kOutput, calls=%fused_computation.6 | convolution fusion | flops 4026531840 | bytes 12845056 | tf_op jit(solution)/shard_map/dot_general | solution.py:274
  150.8 3.2 %fusion.13 = f32[640,640]{1,0:T(8,128)S(1)} fusion(bf16[640,3072]{1,0:T(8,128)(2,1)S(1)} %copy-done.1), kind=kOutput, calls=%fused_computation.46 | convolution fusion | flops 2516582400 | bytes 5570560 | tf_op jit(solution)/shard_map/dot_general | solution.py:137
  154.1 6.8 %fusion.2 = f32[640,1024]{1,0:T(8,128)S(1)} fusion(bf16[640,3072]{1,0:T(8,128)(2,1)S(1)} %copy-done.1, bf16[3072,3072]{1,0:T(8,128)(2,1)} %param.12), kind=kOutput, calls=%fused_computation.4 | convolution fusion | flops 4026531840 | bytes 12845056 | tf_op jit(solution)/shard_map/dot_general | solution.py:274
  162.8 6.6 %fusion = f32[640,1024]{1,0:T(8,128)S(1)} fusion(bf16[640,3072]{1,0:T(8,128)(2,1)S(1)} %copy-done.1, bf16[3072,3072]{1,0:T(8,128)(2,1)} %param.12), kind=kOutput, calls=%fused_computation.2 | convolution fusion | flops 4026531840 | bytes 12845056 | tf_op jit(solution)/shard_map/dot_general | solution.py:274
  170.9 4.4 %shard_map.99 = bf16[640,3072]{1,0:T(8,128)(2,1)} custom-call(s32[3]{0:T(128)} %pad_add_fusion.flags_ref, bf16[80,3072]{1,0:T(8,128)(2,1)} %refs_0_.1, bf16[80,3072]{1,0:T(8,128)(2,1)} %collective-permute-done.13.refs_1_, bf16[80,3072]{1,0:T(8,128)(2,1)} %collective-permute-done.14.refs_2_, bf16[80,3072]{1,0:T(8,128)(2,1)} %collective-permute-done.18.refs_3_, ...), custom_call_target="tpu_custom_call" | custom-call | flops 1000 | bytes 11796480 | tf_op jit(solution)/shard_map/pallas_call | solution.py:126
  175.2 7.2 %multiply_reduce_fusion = f32[]{:T(128)} fusion(f32[640,640]{1,0:T(8,128)S(1)} %fusion.13, bf16[640,3072]{1,0:T(8,128)(2,1)} %shard_map.99), kind=kOutput, calls=%fused_computation.14 | convolution fusion | flops 2517401600 | bytes 5570564 | tf_op jit(solution)/shard_map/dot_general | solution.py:137
  185.6 3.1 %collective-permute-done.25 = f32[3]{0:T(128)S(1)} collective-permute-done((f32[3]{0:T(128)S(1)}, f32[3]{0:T(128)S(1)}, u32[]{:S(2)}, u32[]{:S(2)}) %collective-permute-start.25) | collective-permute-done | bytes 44 | tf_op jit(solution)/shard_map/ppermute | solution.py:21
  189.2 3.0 %collective-permute-done.26 = f32[3]{0:T(128)S(1)} collective-permute-done((f32[3]{0:T(128)S(1)}, f32[3]{0:T(128)S(1)}, u32[]{:S(2)}, u32[]{:S(2)}) %collective-permute-start.26) | collective-permute-done | bytes 44 | tf_op jit(solution)/shard_map/ppermute | solution.py:21
  211.0 17.9 %multiply_convert_fusion.1 = bf16[3072,3072]{1,0:T(8,128)(2,1)} fusion(f32[]{:T(128)S(6)} %div.23, bf16[640,3072]{1,0:T(8,128)(2,1)S(1)} %copy-done.21, bf16[640,3072]{1,0:T(8,128)(2,1)S(1)} %copy-done), kind=kOutput, calls=%fused_computation.1 | convolution fusion | flops 12098469888 | bytes 26738692 | tf_op jit(solution)/shard_map/dot_general | solution.py:316
  235.0 17.9 %multiply_convert_fusion = bf16[3072,3072]{1,0:T(8,128)(2,1)} fusion(f32[]{:T(128)S(6)} %div.23, bf16[640,3072]{1,0:T(8,128)(2,1)S(1)} %copy-done.3, bf16[640,3072]{1,0:T(8,128)(2,1)S(1)} %copy-done.2), kind=kOutput, calls=%fused_computation | convolution fusion | flops 12098469888 | bytes 26738692 | tf_op jit(solution)/shard_map/dot_general | solution.py:316
  (149 shorter events, 68.3 us)
Async XLA Ops:
  5.5 15.1 %collective-permute-start = (bf16[80,3072]{1,0:T(8,128)(2,1)S(1)}, bf16[80,3072]{1,0:T(8,128)(2,1)S(1)}, u32[]{:S(2)}, u32[]{:S(2)}) collective-permute-start(bf16[80,3072]{1,0:T(8,128)(2,1)S(1)} %broadcast_multiply_fusion.refs_0_), channel_id=1, source_target_pairs={{0,4},{4,0},{8,12},{12,8},{16,20},{20,16},{24,28},{28,24},{1,5},{5... | collective-permute-start | bytes 1474568 | tf_op jit(solution)/shard_map/ppermute | solution.py:21
  18.4 25.9 %collective-permute-start.4 = (bf16[160,3072]{1,0:T(8,128)(2,1)}, bf16[160,3072]{1,0:T(8,128)(2,1)}, u32[]{:S(2)}, u32[]{:S(2)}) collective-permute-start(bf16[160,3072]{1,0:T(8,128)(2,1)} %refs_0_), channel_id=1, source_target_pairs={{0,2},{1,3},{2,0},{3,1},{4,6},{5,7},{6,4},{7,5},{8,10},{9,11},{10,... | collective-permute-start | bytes 2949128 | tf_op jit(solution)/shard_map/ppermute | solution.py:21
  20.6 23.7 %collective-permute-start.3 = (bf16[80,3072]{1,0:T(8,128)(2,1)S(1)}, bf16[80,3072]{1,0:T(8,128)(2,1)}, u32[]{:S(2)}, u32[]{:S(2)}) collective-permute-start(bf16[80,3072]{1,0:T(8,128)(2,1)S(1)} %broadcast_multiply_fusion.refs_0_), channel_id=1, source_target_pairs={{0,16},{4,20},{8,24},{12,28},{16,0},{20,4},{24,8},{28,12},{1,17},{... | collective-permute-start | bytes 1474568 | tf_op jit(solution)/shard_map/ppermute | solution.py:21
  44.9 18.8 %collective-permute-start.11 = (bf16[80,3072]{1,0:T(8,128)(2,1)}, bf16[80,3072]{1,0:T(8,128)(2,1)}, u32[]{:S(2)}, u32[]{:S(2)}) collective-permute-start(bf16[80,3072]{1,0:T(8,128)(2,1)} %collective-permute-done.3.refs_0_), channel_id=1, source_target_pairs={{0,8},{4,12},{8,0},{12,4},{16,24},{20,28},{24,16},{28,20},{1,9},{5... | collective-permute-start | bytes 1474568 | tf_op jit(solution)/shard_map/ppermute | solution.py:21
  46.4 17.4 %collective-permute-start.10 = (bf16[80,3072]{1,0:T(8,128)(2,1)}, bf16[80,3072]{1,0:T(8,128)(2,1)}, u32[]{:S(2)}, u32[]{:S(2)}) collective-permute-start(bf16[80,3072]{1,0:T(8,128)(2,1)} %collective-permute-done.3.refs_0_), channel_id=1, source_target_pairs={{0,4},{4,0},{8,12},{12,8},{16,20},{20,16},{24,28},{28,24},{1,5},{5... | collective-permute-start | bytes 1474568 | tf_op jit(solution)/shard_map/ppermute | solution.py:21
  48.2 33.3 %collective-permute-start.6 = (bf16[160,3072]{1,0:T(8,128)(2,1)S(1)}, bf16[160,3072]{1,0:T(8,128)(2,1)S(1)}, u32[]{:S(2)}, u32[]{:S(2)}) collective-permute-start(bf16[160,3072]{1,0:T(8,128)(2,1)S(1)} %get-tuple-element.53), channel_id=1, source_target_pairs={{0,2},{1,3},{2,0},{3,1},{4,6},{5,7},{6,4},{7,5},{8,10},{9,11},{10,... | collective-permute-start | bytes 2949128 | tf_op jit(solution)/shard_map/ppermute | solution.py:21
  64.4 28.1 %collective-permute-start.15 = (bf16[80,3072]{1,0:T(8,128)(2,1)}, bf16[80,3072]{1,0:T(8,128)(2,1)}, u32[]{:S(2)}, u32[]{:S(2)}) collective-permute-start(bf16[80,3072]{1,0:T(8,128)(2,1)} %refs_0_.1), channel_id=1, source_target_pairs={{0,16},{4,20},{8,24},{12,28},{16,0},{20,4},{24,8},{28,12},{1,17},{... | collective-permute-start | bytes 1474568 | tf_op jit(solution)/shard_map/ppermute | solution.py:21
  67.0 25.6 %collective-permute-start.14 = (bf16[80,3072]{1,0:T(8,128)(2,1)}, bf16[80,3072]{1,0:T(8,128)(2,1)}, u32[]{:S(2)}, u32[]{:S(2)}) collective-permute-start(bf16[80,3072]{1,0:T(8,128)(2,1)} %refs_0_.1), channel_id=1, source_target_pairs={{0,8},{4,12},{8,0},{12,4},{16,24},{20,28},{24,16},{28,20},{1,9},{5... | collective-permute-start | bytes 1474568 | tf_op jit(solution)/shard_map/ppermute | solution.py:21
  77.4 15.2 %collective-permute-start.13 = (bf16[80,3072]{1,0:T(8,128)(2,1)}, bf16[80,3072]{1,0:T(8,128)(2,1)}, u32[]{:S(2)}, u32[]{:S(2)}) collective-permute-start(bf16[80,3072]{1,0:T(8,128)(2,1)} %refs_0_.1), channel_id=1, source_target_pairs={{0,4},{4,0},{8,12},{12,8},{16,20},{20,16},{24,28},{28,24},{1,5},{5... | collective-permute-start | bytes 1474568 | tf_op jit(solution)/shard_map/ppermute | solution.py:21
  93.1 29.9 %collective-permute-start.9 = (bf16[160,3072]{1,0:T(8,128)(2,1)S(1)}, bf16[160,3072]{1,0:T(8,128)(2,1)S(1)}, u32[]{:S(2)}, u32[]{:S(2)}) collective-permute-start(bf16[160,3072]{1,0:T(8,128)(2,1)S(1)} %multiply_convert_fusion.3.refs_0_), channel_id=1, source_target_pairs={{0,1},{1,0},{2,3},{3,2},{4,5},{5,4},{6,7},{7,6},{8,9},{9,8},{10,11... | collective-permute-start | bytes 2949128 | tf_op jit(solution)/shard_map/ppermute | solution.py:21
  96.5 26.4 %collective-permute-start.17 = (bf16[160,3072]{1,0:T(8,128)(2,1)}, bf16[160,3072]{1,0:T(8,128)(2,1)}, u32[]{:S(2)}, u32[]{:S(2)}) collective-permute-start(bf16[160,3072]{1,0:T(8,128)(2,1)} %get-tuple-element.51), channel_id=1, source_target_pairs={{0,2},{1,3},{2,0},{3,1},{4,6},{5,7},{6,4},{7,5},{8,10},{9,11},{10,... | collective-permute-start | bytes 2949128 | tf_op jit(solution)/shard_map/ppermute | solution.py:21
  97.8 29.1 %collective-permute-start.22 = (bf16[80,3072]{1,0:T(8,128)(2,1)}, bf16[80,3072]{1,0:T(8,128)(2,1)}, u32[]{:S(2)}, u32[]{:S(2)}) collective-permute-start(bf16[80,3072]{1,0:T(8,128)(2,1)} %collective-permute-done.15.refs_4_), channel_id=1, source_target_pairs={{0,8},{4,12},{8,0},{12,4},{16,24},{20,28},{24,16},{28,20},{1,9},{5... | collective-permute-start | bytes 1474568 | tf_op jit(solution)/shard_map/ppermute | solution.py:21
  99.4 23.6 %collective-permute-start.19 = (bf16[80,3072]{1,0:T(8,128)(2,1)}, bf16[80,3072]{1,0:T(8,128)(2,1)}, u32[]{:S(2)}, u32[]{:S(2)}) collective-permute-start(bf16[80,3072]{1,0:T(8,128)(2,1)} %collective-permute-done.15.refs_4_), channel_id=1, source_target_pairs={{0,4},{4,0},{8,12},{12,8},{16,20},{20,16},{24,28},{28,24},{1,5},{5... | collective-permute-start | bytes 1474568 | tf_op jit(solution)/shard_map/ppermute | solution.py:21
  100.1 22.8 %collective-permute-start.18 = (bf16[80,3072]{1,0:T(8,128)(2,1)}, bf16[80,3072]{1,0:T(8,128)(2,1)}, u32[]{:S(2)}, u32[]{:S(2)}) collective-permute-start(bf16[80,3072]{1,0:T(8,128)(2,1)} %collective-permute-done.14.refs_2_), channel_id=1, source_target_pairs={{0,4},{4,0},{8,12},{12,8},{16,20},{20,16},{24,28},{28,24},{1,5},{5... | collective-permute-start | bytes 1474568 | tf_op jit(solution)/shard_map/ppermute | solution.py:21
  126.9 27.2 %collective-permute-start.23 = (bf16[80,3072]{1,0:T(8,128)(2,1)}, bf16[80,3072]{1,0:T(8,128)(2,1)S(1)}, u32[]{:S(2)}, u32[]{:S(2)}) collective-permute-start(bf16[80,3072]{1,0:T(8,128)(2,1)} %collective-permute-done.22.refs_6_), channel_id=1, source_target_pairs={{0,4},{4,0},{8,12},{12,8},{16,20},{20,16},{24,28},{28,24},{1,5},{5... | collective-permute-start | bytes 1474568 | tf_op jit(solution)/shard_map/ppermute | solution.py:21
  149.6 53.6 %collective-permute-start.21 = (bf16[320,1024]{1,0:T(8,128)(2,1)}, bf16[320,1024]{1,0:T(8,128)(2,1)}, u32[]{:S(2)}, u32[]{:S(2)}) collective-permute-start(bf16[320,1024]{1,0:T(8,128)(2,1)} %slice.187), channel_id=1, source_target_pairs={{0,4},{4,0},{8,12},{12,8},{16,20},{20,16},{24,28},{28,24},{1,5},{5... | collective-permute-start | bytes 1966088 | tf_op jit(solution)/shard_map/ppermute | solution.py:21
  162.0 41.1 %collective-permute-start.30 = (bf16[320,1024]{1,0:T(8,128)(2,1)}, bf16[320,1024]{1,0:T(8,128)(2,1)}, u32[]{:S(2)}, u32[]{:S(2)}) collective-permute-start(bf16[320,1024]{1,0:T(8,128)(2,1)} %slice.186), channel_id=1, source_target_pairs={{0,4},{4,0},{8,12},{12,8},{16,20},{20,16},{24,28},{28,24},{1,5},{5... | collective-permute-start | bytes 1966088 | tf_op jit(solution)/shard_map/ppermute | solution.py:21
  169.5 39.6 %collective-permute-start.33 = (bf16[320,1024]{1,0:T(8,128)(2,1)S(1)}, bf16[320,1024]{1,0:T(8,128)(2,1)}, u32[]{:S(2)}, u32[]{:S(2)}) collective-permute-start(bf16[320,1024]{1,0:T(8,128)(2,1)S(1)} %slice.185), channel_id=1, source_target_pairs={{0,4},{4,0},{8,12},{12,8},{16,20},{20,16},{24,28},{28,24},{1,5},{5... | collective-permute-start | bytes 1966088 | tf_op jit(solution)/shard_map/ppermute | solution.py:21
  207.0 21.9 %collective-permute-start.31 = (bf16[160,1024]{1,0:T(8,128)(2,1)S(1)}, bf16[160,1024]{1,0:T(8,128)(2,1)S(1)}, u32[]{:S(2)}, u32[]{:S(2)}) collective-permute-start(bf16[160,1024]{1,0:T(8,128)(2,1)S(1)} %slice.189), channel_id=1, source_target_pairs={{0,8},{4,12},{8,0},{12,4},{16,24},{20,28},{24,16},{28,20},{1,9},{5... | collective-permute-start | bytes 983048 | tf_op jit(solution)/shard_map/ppermute | solution.py:21
  207.6 24.1 %collective-permute-start.28 = (bf16[160,1024]{1,0:T(8,128)(2,1)S(1)}, bf16[160,1024]{1,0:T(8,128)(2,1)S(1)}, u32[]{:S(2)}, u32[]{:S(2)}) collective-permute-start(bf16[160,1024]{1,0:T(8,128)(2,1)S(1)} %slice.190), channel_id=1, source_target_pairs={{0,8},{4,12},{8,0},{12,4},{16,24},{20,28},{24,16},{28,20},{1,9},{5... | collective-permute-start | bytes 983048 | tf_op jit(solution)/shard_map/ppermute | solution.py:21
  210.4 21.8 %collective-permute-start.34 = (bf16[160,1024]{1,0:T(8,128)(2,1)S(1)}, bf16[160,1024]{1,0:T(8,128)(2,1)S(1)}, u32[]{:S(2)}, u32[]{:S(2)}) collective-permute-start(bf16[160,1024]{1,0:T(8,128)(2,1)S(1)} %slice.188), channel_id=1, source_target_pairs={{0,8},{4,12},{8,0},{12,4},{16,24},{20,28},{24,16},{28,20},{1,9},{5... | collective-permute-start | bytes 983048 | tf_op jit(solution)/shard_map/ppermute | solution.py:21
  229.0 23.9 %collective-permute-start.32 = (bf16[80,1024]{1,0:T(8,128)(2,1)S(1)}, bf16[80,1024]{1,0:T(8,128)(2,1)S(1)}, u32[]{:S(2)}, u32[]{:S(2)}) collective-permute-start(bf16[80,1024]{1,0:T(8,128)(2,1)S(1)} %slice.192), channel_id=1, source_target_pairs={{0,16},{4,20},{8,24},{12,28},{16,0},{20,4},{24,8},{28,12},{1,17},{... | collective-permute-start | bytes 491528 | tf_op jit(solution)/shard_map/ppermute | solution.py:21
  231.8 21.1 %collective-permute-start.29 = (bf16[80,1024]{1,0:T(8,128)(2,1)S(1)}, bf16[80,1024]{1,0:T(8,128)(2,1)S(1)}, u32[]{:S(2)}, u32[]{:S(2)}) collective-permute-start(bf16[80,1024]{1,0:T(8,128)(2,1)S(1)} %slice.193), channel_id=1, source_target_pairs={{0,16},{4,20},{8,24},{12,28},{16,0},{20,4},{24,8},{28,12},{1,17},{... | collective-permute-start | bytes 491528 | tf_op jit(solution)/shard_map/ppermute | solution.py:21
  232.3 20.7 %collective-permute-start.35 = (bf16[80,1024]{1,0:T(8,128)(2,1)S(1)}, bf16[80,1024]{1,0:T(8,128)(2,1)S(1)}, u32[]{:S(2)}, u32[]{:S(2)}) collective-permute-start(bf16[80,1024]{1,0:T(8,128)(2,1)S(1)} %slice.191), channel_id=1, source_target_pairs={{0,16},{4,20},{8,24},{12,28},{16,0},{20,4},{24,8},{28,12},{1,17},{... | collective-permute-start | bytes 491528 | tf_op jit(solution)/shard_map/ppermute | solution.py:21
  (36 other events, 279.2 us)
where the time goes:
time: 255 us; the launch traced here: 254 us
  matrix products  105 us (41%)
  waiting for transfers between devices  48.4 us (19%)
  starting transfers between devices  43.3 us (17%)
  Pallas kernels  31.6 us (12%)
  other arithmetic  12.9 us (5%)
  local copies, waits for them, and re-layouts  6.95 us (3%)
  between operations  6.05 us (2%)
    ppermute x37, waiting for transfers between devices, swap(): return lax.ppermute(value, axis, [(i, i ^ bit) for i in range(size)])  48.4 us
    ppermute x37, starting transfers between devices, swap(): return lax.ppermute(value, axis, [(i, i ^ bit) for i in range(size)])  43.3 us
    dot_general x2, matrix products, gradient(): product = lax.dot_general(left, right, FIRST, preferred_element_type=F32)  35.8 us
    dot_general x4, matrix products, gram(): return lax.dot_general(value, value, LAST, preferred_element_type=F32)  26 us
    dot_general x2, matrix products, on_device(): lax.dot_general(after(block, *first), w_down, LAST, preferred_element_typ...  21.8 us
    dot_general x3, matrix products, on_device(): lax.dot_general(operand, w_up[part * step:(part + 1) * step], LAST, prefe...  21.1 us
    pallas_call x5, Pallas kernels, arrange(): call(kernel, (width // tile,), [pl.BlockSpec((piece.shape[0], tile), colu...  19.6 us
    pallas_call x1, Pallas kernels, gelu_all(): call(kernel, (width // tile,), [pl.BlockSpec((piece.shape[0], tile), colu...  12 us
  transfers between devices with their start and end apart: 37, of which 11 were waited for; matrix products, arithmetic and copies ran while one was open for 47% of the time, Pallas kernels for 12%

commit v1 on v0

--- a/solution.py
+++ b/solution.py
@@ -289,15 +289,16 @@
     scalars = jnp.stack([count_term, keep_block * (square_down + square_up), flag_value])
     for bit in col_bits:
         scalars = scalars + swap(scalars, "col", bit)
+    col_sums = scalars
     for bit in row_bits[1:]:
         scalars = scalars + swap(scalars, "row", bit)
     stages = []
     for total, got in sums:
-        stages.append([total + after(got, scalars).astype(F32)])
+        stages.append([total + after(got, col_sums).astype(F32)])
         for bit in row_bits[1:]:
             total = stages[-1][-1]
             split = total.shape[0] // 2
-            got = swap(total[split:].astype(BF16), "row", bit)
+            got = swap(after(total[split:].astype(BF16), scalars), "row", bit)
             stages[-1].append(total[:split] + got.astype(F32))
     scalars = scalars + swap(scalars, "row", 1)
     count_all, square_all, flag_all = scalars[0], jnp.maximum(scalars[1], 0.0), scalars[2]

time: 255 us -> 255 us (level)
  no operation moved by 1% of the time
where the time goes in v1:
time: 255 us; the launch traced here: 254 us
  matrix products  105 us (41%)
  waiting for transfers between devices  48.4 us (19%)
  starting transfers between devices  43.3 us (17%)
  Pallas kernels  31.6 us (12%)
  other arithmetic  12.9 us (5%)
  local copies, waits for them, and re-layouts  6.95 us (3%)
  between operations  6.05 us (2%)
    ppermute x37, waiting for transfers between devices, swap(): return lax.ppermute(value, axis, [(i, i ^ bit) for i in range(size)])  48.4 us
    ppermute x37, starting transfers between devices, swap(): return lax.ppermute(value, axis, [(i, i ^ bit) for i in range(size)])  43.3 us
    dot_general x2, matrix products, gradient(): product = lax.dot_general(left, right, FIRST, preferred_element_type=F32)  35.8 us
    dot_general x4, matrix products, gram(): return lax.dot_general(value, value, LAST, preferred_element_type=F32)  26 us
    dot_general x2, matrix products, on_device(): lax.dot_general(after(block, *first), w_down, LAST, preferred_element_typ...  21.8 us
    dot_general x3, matrix products, on_device(): lax.dot_general(operand, w_up[part * step:(part + 1) * step], LAST, prefe...  21.1 us
    pallas_call x5, Pallas kernels, arrange(): call(kernel, (width // tile,), [pl.BlockSpec((piece.shape[0], tile), colu...  19.6 us
    pallas_call x1, Pallas kernels, gelu_all(): call(kernel, (width // tile,), [pl.BlockSpec((piece.shape[0], tile), colu...  12 us
  transfers between devices with their start and end apart: 37, of which 11 were waited for; matrix products, arithmetic and copies ran while one was open for 47% of the time, Pallas kernels for 12%

profile of v1, /device:TPU:0, one launch (start us, length us, event | category | flops | bytes accessed | tf_op | source)
XLA Modules:
  0.0 253.9 jit_solution(7957003879711554056)
XLA Ops:
  2.4 3.1 %collective-permute-start.1 = (bf16[80,3072]{1,0:T(8,128)(2,1)S(1)}, bf16[80,3072]{1,0:T(8,128)(2,1)S(1)}, u32[]{:S(2)}, u32[]{:S(2)}) collective-permute-start(bf16[80,3072]{1,0:T(8,128)(2,1)S(1)} %broadcast_multiply_fusion.refs_0_), channel_id=1, source_target_pairs={{0,8},{4,12},{8,0},{12,4},{16,24},{20,28},{24,16},{28,20},{1,9},{5... | collective-permute-start | bytes 1474568 | tf_op jit(solution)/shard_map/ppermute | solution.py:21
  7.0 9.7 %collective-permute-done.1.refs_2_ = bf16[80,3072]{1,0:T(8,128)(2,1)S(1)} collective-permute-done((bf16[80,3072]{1,0:T(8,128)(2,1)S(1)}, bf16[80,3072]{1,0:T(8,128)(2,1)S(1)}, u32[]{:S(2)}, u32[]{:S(2)}) %collective-permute-start.1) | collective-permute-done | bytes 491552 | tf_op jit(solution)/shard_map/ppermute | solution.py:21
  23.2 6.0 %collective-permute-done.2.refs_3_ = bf16[80,3072]{1,0:T(8,128)(2,1)S(1)} collective-permute-done((bf16[80,3072]{1,0:T(8,128)(2,1)S(1)}, bf16[80,3072]{1,0:T(8,128)(2,1)S(1)}, u32[]{:S(2)}, u32[]{:S(2)}) %collective-permute-start.2) | collective-permute-done | bytes 491552 | tf_op jit(solution)/shard_map/ppermute | solution.py:21
  30.0 3.4 %shard_map.94.refs_0_ = bf16[320,3072]{1,0:T(8,128)(2,1)} custom-call(s32[3]{0:T(128)} %pad_add_fusion.flags_ref, bf16[80,3072]{1,0:T(8,128)(2,1)} %copy-done.7, bf16[80,3072]{1,0:T(8,128)(2,1)} %copy-done.17, bf16[80,3072]{1,0:T(8,128)(2,1)} %copy-done.16, bf16[80,3072]{1,0:T(8,128)(2,1)} %copy-done.18), custom_call_target="tpu_custom_call" | custom-call | flops 1000 | bytes 5898240 | tf_op jit(solution)/shard_map/pallas_call | solution.py:126
  33.4 10.8 %fusion.10 = f32[320,3072]{1,0:T(8,128)S(1)} fusion(bf16[320,3072]{1,0:T(8,128)(2,1)} %shard_map.94.refs_0_, bf16[3072,3072]{1,0:T(8,128)(2,1)} %param.13), kind=kOutput, calls=%fused_computation.43 | convolution fusion | flops 6039797760 | bytes 24772608 | tf_op jit(solution)/shard_map/dot_general | solution.py:219
  51.7 12.0 %shard_map.95 = (bf16[640,3072]{1,0:T(8,128)(2,1)}, f32[320,3072]{1,0:T(8,128)}) custom-call(s32[3]{0:T(128)} %pad_add_fusion.flags_ref, bf16[160,3072]{1,0:T(8,128)(2,1)} %refs_0_, bf16[160,3072]{1,0:T(8,128)(2,1)} %collective-permute-done.4.refs_1_, bf16[160,3072]{1,0:T(8,128)(2,1)} %copy-done.14, bf16[160,3072]{1,0:T(8,128)(2,1)} %copy-done.15), custom_call_target="tpu_custom_call" | custom-call | flops 1000 | bytes 47185920 | tf_op jit(solution)/shard_map/pallas_call | solution.py:99
  68.6 8.8 %collective-permute-done.12.refs_3_ = bf16[80,3072]{1,0:T(8,128)(2,1)S(1)} collective-permute-done((bf16[80,3072]{1,0:T(8,128)(2,1)}, bf16[80,3072]{1,0:T(8,128)(2,1)S(1)}, u32[]{:S(2)}, u32[]{:S(2)}) %collective-permute-start.12) | collective-permute-done | bytes 491552 | tf_op jit(solution)/shard_map/ppermute | solution.py:21
  78.1 3.4 %shard_map.96.refs_1_ = bf16[320,3072]{1,0:T(8,128)(2,1)} custom-call(s32[3]{0:T(128)} %pad_add_fusion.flags_ref, bf16[80,3072]{1,0:T(8,128)(2,1)} %collective-permute-done.3.refs_0_, bf16[80,3072]{1,0:T(8,128)(2,1)} %collective-permute-done.10.refs_1_, bf16[80,3072]{1,0:T(8,128)(2,1)} %collective-permute-done.11.refs_2_, bf16[80,3072]{1,0:T(8,128)(2,1)} %copy-done.20), custom_call_target="tpu_custom_call" | custom-call | flops 1000 | bytes 5898240 | tf_op jit(solution)/shard_map/pallas_call | solution.py:126
  81.5 10.9 %fusion.11 = f32[320,3072]{1,0:T(8,128)S(1)} fusion(bf16[320,3072]{1,0:T(8,128)(2,1)} %shard_map.96.refs_1_, bf16[3072,3072]{1,0:T(8,128)(2,1)} %param.13), kind=kOutput, calls=%fused_computation.44 | convolution fusion | flops 6039797760 | bytes 24772608 | tf_op jit(solution)/shard_map/dot_general | solution.py:219
  101.4 4.3 %shard_map.97 = bf16[640,3072]{1,0:T(8,128)(2,1)} custom-call(s32[3]{0:T(128)} %pad_add_fusion.flags_ref, bf16[320,3072]{1,0:T(8,128)(2,1)} %shard_map.94.refs_0_, bf16[320,3072]{1,0:T(8,128)(2,1)} %shard_map.96.refs_1_), custom_call_target="tpu_custom_call" | custom-call | flops 1000 | bytes 11796480 | tf_op jit(solution)/shard_map/pallas_call | solution.py:126
  105.7 7.7 %fusion.12 = f32[640,640]{1,0:T(8,128)} fusion(bf16[640,3072]{1,0:T(8,128)(2,1)} %shard_map.97), kind=kOutput, calls=%fused_computation.45 | convolution fusion | flops 2516582400 | bytes 5570560 | tf_op jit(solution)/shard_map/dot_general | solution.py:137
  113.4 9.5 %collective-permute-done.18.refs_3_ = bf16[80,3072]{1,0:T(8,128)(2,1)} collective-permute-done((bf16[80,3072]{1,0:T(8,128)(2,1)}, bf16[80,3072]{1,0:T(8,128)(2,1)}, u32[]{:S(2)}, u32[]{:S(2)}) %collective-permute-start.18) | collective-permute-done | bytes 491552 | tf_op jit(solution)/shard_map/ppermute | solution.py:21
  127.8 7.8 %multiply_reduce_fusion.1 = f32[]{:T(128)} fusion(f32[640,640]{1,0:T(8,128)} %fusion.12, bf16[640,3072]{1,0:T(8,128)(2,1)} %get-tuple-element.47), kind=kOutput, calls=%fused_computation.15 | convolution fusion | flops 2517401600 | bytes 5570564 | tf_op jit(solution)/shard_map/dot_general | solution.py:137
  136.5 4.2 %shard_map.98 = bf16[640,3072]{1,0:T(8,128)(2,1)} custom-call(s32[3]{0:T(128)} %pad_add_fusion.flags_ref, bf16[160,3072]{1,0:T(8,128)(2,1)} %copy-done.5, bf16[160,3072]{1,0:T(8,128)(2,1)} %copy-done.11, bf16[160,3072]{1,0:T(8,128)(2,1)} %copy-done.6, bf16[160,3072]{1,0:T(8,128)(2,1)} %copy-done.12), custom_call_target="tpu_custom_call" | custom-call | flops 1000 | bytes 11796480 | tf_op jit(solution)/shard_map/pallas_call | solution.py:126
  140.7 7.7 %fusion.4 = f32[640,1024]{1,0:T(8,128)S(1)} fusion(bf16[640,3072]{1,0:T(8,128)(2,1)} %shard_map.98, bf16[3072,3072]{1,0:T(8,128)(2,1)} %param.12), kind=kOutput, calls=%fused_computation.6 | convolution fusion | flops 4026531840 | bytes 12845056 | tf_op jit(solution)/shard_map/dot_general | solution.py:274
  150.8 3.2 %fusion.13 = f32[640,640]{1,0:T(8,128)S(1)} fusion(bf16[640,3072]{1,0:T(8,128)(2,1)S(1)} %copy-done.1), kind=kOutput, calls=%fused_computation.46 | convolution fusion | flops 2516582400 | bytes 5570560 | tf_op jit(solution)/shard_map/dot_general | solution.py:137
  154.1 6.8 %fusion.2 = f32[640,1024]{1,0:T(8,128)S(1)} fusion(bf16[640,3072]{1,0:T(8,128)(2,1)S(1)} %copy-done.1, bf16[3072,3072]{1,0:T(8,128)(2,1)} %param.12), kind=kOutput, calls=%fused_computation.4 | convolution fusion | flops 4026531840 | bytes 12845056 | tf_op jit(solution)/shard_map/dot_general | solution.py:274
  162.8 6.6 %fusion = f32[640,1024]{1,0:T(8,128)S(1)} fusion(bf16[640,3072]{1,0:T(8,128)(2,1)S(1)} %copy-done.1, bf16[3072,3072]{1,0:T(8,128)(2,1)} %param.12), kind=kOutput, calls=%fused_computation.2 | convolution fusion | flops 4026531840 | bytes 12845056 | tf_op jit(solution)/shard_map/dot_general | solution.py:274
  170.9 4.4 %shard_map.99 = bf16[640,3072]{1,0:T(8,128)(2,1)} custom-call(s32[3]{0:T(128)} %pad_add_fusion.flags_ref, bf16[80,3072]{1,0:T(8,128)(2,1)} %refs_0_.1, bf16[80,3072]{1,0:T(8,128)(2,1)} %collective-permute-done.13.refs_1_, bf16[80,3072]{1,0:T(8,128)(2,1)} %collective-permute-done.14.refs_2_, bf16[80,3072]{1,0:T(8,128)(2,1)} %collective-permute-done.18.refs_3_, ...), custom_call_target="tpu_custom_call" | custom-call | flops 1000 | bytes 11796480 | tf_op jit(solution)/shard_map/pallas_call | solution.py:126
  175.2 7.2 %multiply_reduce_fusion = f32[]{:T(128)} fusion(f32[640,640]{1,0:T(8,128)S(1)} %fusion.13, bf16[640,3072]{1,0:T(8,128)(2,1)} %shard_map.99), kind=kOutput, calls=%fused_computation.14 | convolution fusion | flops 2517401600 | bytes 5570564 | tf_op jit(solution)/shard_map/dot_general | solution.py:137
  185.6 3.1 %collective-permute-done.25 = f32[3]{0:T(128)S(1)} collective-permute-done((f32[3]{0:T(128)S(1)}, f32[3]{0:T(128)S(1)}, u32[]{:S(2)}, u32[]{:S(2)}) %collective-permute-start.25) | collective-permute-done | bytes 44 | tf_op jit(solution)/shard_map/ppermute | solution.py:21
  189.2 3.0 %collective-permute-done.26 = f32[3]{0:T(128)S(1)} collective-permute-done((f32[3]{0:T(128)S(1)}, f32[3]{0:T(128)S(1)}, u32[]{:S(2)}, u32[]{:S(2)}) %collective-permute-start.26) | collective-permute-done | bytes 44 | tf_op jit(solution)/shard_map/ppermute | solution.py:21
  211.0 17.9 %multiply_convert_fusion.1 = bf16[3072,3072]{1,0:T(8,128)(2,1)} fusion(f32[]{:T(128)S(6)} %div.23, bf16[640,3072]{1,0:T(8,128)(2,1)S(1)} %copy-done.21, bf16[640,3072]{1,0:T(8,128)(2,1)S(1)} %copy-done), kind=kOutput, calls=%fused_computation.1 | convolution fusion | flops 12098469888 | bytes 26738692 | tf_op jit(solution)/shard_map/dot_general | solution.py:317
  235.0 17.9 %multiply_convert_fusion = bf16[3072,3072]{1,0:T(8,128)(2,1)} fusion(f32[]{:T(128)S(6)} %div.23, bf16[640,3072]{1,0:T(8,128)(2,1)S(1)} %copy-done.3, bf16[640,3072]{1,0:T(8,128)(2,1)S(1)} %copy-done.2), kind=kOutput, calls=%fused_computation | convolution fusion | flops 12098469888 | bytes 26738692 | tf_op jit(solution)/shard_map/dot_general | solution.py:317
  (149 shorter events, 68.3 us)
Async XLA Ops:
  5.5 15.1 %collective-permute-start = (bf16[80,3072]{1,0:T(8,128)(2,1)S(1)}, bf16[80,3072]{1,0:T(8,128)(2,1)S(1)}, u32[]{:S(2)}, u32[]{:S(2)}) collective-permute-start(bf16[80,3072]{1,0:T(8,128)(2,1)S(1)} %broadcast_multiply_fusion.refs_0_), channel_id=1, source_target_pairs={{0,4},{4,0},{8,12},{12,8},{16,20},{20,16},{24,28},{28,24},{1,5},{5... | collective-permute-start | bytes 1474568 | tf_op jit(solution)/shard_map/ppermute | solution.py:21
  18.4 25.9 %collective-permute-start.4 = (bf16[160,3072]{1,0:T(8,128)(2,1)}, bf16[160,3072]{1,0:T(8,128)(2,1)}, u32[]{:S(2)}, u32[]{:S(2)}) collective-permute-start(bf16[160,3072]{1,0:T(8,128)(2,1)} %refs_0_), channel_id=1, source_target_pairs={{0,2},{1,3},{2,0},{3,1},{4,6},{5,7},{6,4},{7,5},{8,10},{9,11},{10,... | collective-permute-start | bytes 2949128 | tf_op jit(solution)/shard_map/ppermute | solution.py:21
  20.6 23.7 %collective-permute-start.3 = (bf16[80,3072]{1,0:T(8,128)(2,1)S(1)}, bf16[80,3072]{1,0:T(8,128)(2,1)}, u32[]{:S(2)}, u32[]{:S(2)}) collective-permute-start(bf16[80,3072]{1,0:T(8,128)(2,1)S(1)} %broadcast_multiply_fusion.refs_0_), channel_id=1, source_target_pairs={{0,16},{4,20},{8,24},{12,28},{16,0},{20,4},{24,8},{28,12},{1,17},{... | collective-permute-start | bytes 1474568 | tf_op jit(solution)/shard_map/ppermute | solution.py:21
  44.9 18.8 %collective-permute-start.11 = (bf16[80,3072]{1,0:T(8,128)(2,1)}, bf16[80,3072]{1,0:T(8,128)(2,1)}, u32[]{:S(2)}, u32[]{:S(2)}) collective-permute-start(bf16[80,3072]{1,0:T(8,128)(2,1)} %collective-permute-done.3.refs_0_), channel_id=1, source_target_pairs={{0,8},{4,12},{8,0},{12,4},{16,24},{20,28},{24,16},{28,20},{1,9},{5... | collective-permute-start | bytes 1474568 | tf_op jit(solution)/shard_map/ppermute | solution.py:21
  46.4 17.4 %collective-permute-start.10 = (bf16[80,3072]{1,0:T(8,128)(2,1)}, bf16[80,3072]{1,0:T(8,128)(2,1)}, u32[]{:S(2)}, u32[]{:S(2)}) collective-permute-start(bf16[80,3072]{1,0:T(8,128)(2,1)} %collective-permute-done.3.refs_0_), channel_id=1, source_target_pairs={{0,4},{4,0},{8,12},{12,8},{16,20},{20,16},{24,28},{28,24},{1,5},{5... | collective-permute-start | bytes 1474568 | tf_op jit(solution)/shard_map/ppermute | solution.py:21
  48.2 33.3 %collective-permute-start.6 = (bf16[160,3072]{1,0:T(8,128)(2,1)S(1)}, bf16[160,3072]{1,0:T(8,128)(2,1)S(1)}, u32[]{:S(2)}, u32[]{:S(2)}) collective-permute-start(bf16[160,3072]{1,0:T(8,128)(2,1)S(1)} %get-tuple-element.65), channel_id=1, source_target_pairs={{0,2},{1,3},{2,0},{3,1},{4,6},{5,7},{6,4},{7,5},{8,10},{9,11},{10,... | collective-permute-start | bytes 2949128 | tf_op jit(solution)/shard_map/ppermute | solution.py:21
  64.4 28.1 %collective-permute-start.15 = (bf16[80,3072]{1,0:T(8,128)(2,1)}, bf16[80,3072]{1,0:T(8,128)(2,1)}, u32[]{:S(2)}, u32[]{:S(2)}) collective-permute-start(bf16[80,3072]{1,0:T(8,128)(2,1)} %refs_0_.1), channel_id=1, source_target_pairs={{0,16},{4,20},{8,24},{12,28},{16,0},{20,4},{24,8},{28,12},{1,17},{... | collective-permute-start | bytes 1474568 | tf_op jit(solution)/shard_map/ppermute | solution.py:21
  67.0 25.6 %collective-permute-start.14 = (bf16[80,3072]{1,0:T(8,128)(2,1)}, bf16[80,3072]{1,0:T(8,128)(2,1)}, u32[]{:S(2)}, u32[]{:S(2)}) collective-permute-start(bf16[80,3072]{1,0:T(8,128)(2,1)} %refs_0_.1), channel_id=1, source_target_pairs={{0,8},{4,12},{8,0},{12,4},{16,24},{20,28},{24,16},{28,20},{1,9},{5... | collective-permute-start | bytes 1474568 | tf_op jit(solution)/shard_map/ppermute | solution.py:21
  77.4 15.2 %collective-permute-start.13 = (bf16[80,3072]{1,0:T(8,128)(2,1)}, bf16[80,3072]{1,0:T(8,128)(2,1)}, u32[]{:S(2)}, u32[]{:S(2)}) collective-permute-start(bf16[80,3072]{1,0:T(8,128)(2,1)} %refs_0_.1), channel_id=1, source_target_pairs={{0,4},{4,0},{8,12},{12,8},{16,20},{20,16},{24,28},{28,24},{1,5},{5... | collective-permute-start | bytes 1474568 | tf_op jit(solution)/shard_map/ppermute | solution.py:21
  93.1 29.9 %collective-permute-start.9 = (bf16[160,3072]{1,0:T(8,128)(2,1)S(1)}, bf16[160,3072]{1,0:T(8,128)(2,1)S(1)}, u32[]{:S(2)}, u32[]{:S(2)}) collective-permute-start(bf16[160,3072]{1,0:T(8,128)(2,1)S(1)} %multiply_convert_fusion.3.refs_0_), channel_id=1, source_target_pairs={{0,1},{1,0},{2,3},{3,2},{4,5},{5,4},{6,7},{7,6},{8,9},{9,8},{10,11... | collective-permute-start | bytes 2949128 | tf_op jit(solution)/shard_map/ppermute | solution.py:21
  96.5 26.4 %collective-permute-start.17 = (bf16[160,3072]{1,0:T(8,128)(2,1)}, bf16[160,3072]{1,0:T(8,128)(2,1)}, u32[]{:S(2)}, u32[]{:S(2)}) collective-permute-start(bf16[160,3072]{1,0:T(8,128)(2,1)} %get-tuple-element.63), channel_id=1, source_target_pairs={{0,2},{1,3},{2,0},{3,1},{4,6},{5,7},{6,4},{7,5},{8,10},{9,11},{10,... | collective-permute-start | bytes 2949128 | tf_op jit(solution)/shard_map/ppermute | solution.py:21
  97.8 29.1 %collective-permute-start.22 = (bf16[80,3072]{1,0:T(8,128)(2,1)}, bf16[80,3072]{1,0:T(8,128)(2,1)}, u32[]{:S(2)}, u32[]{:S(2)}) collective-permute-start(bf16[80,3072]{1,0:T(8,128)(2,1)} %collective-permute-done.15.refs_4_), channel_id=1, source_target_pairs={{0,8},{4,12},{8,0},{12,4},{16,24},{20,28},{24,16},{28,20},{1,9},{5... | collective-permute-start | bytes 1474568 | tf_op jit(solution)/shard_map/ppermute | solution.py:21
  99.4 23.6 %collective-permute-start.19 = (bf16[80,3072]{1,0:T(8,128)(2,1)}, bf16[80,3072]{1,0:T(8,128)(2,1)}, u32[]{:S(2)}, u32[]{:S(2)}) collective-permute-start(bf16[80,3072]{1,0:T(8,128)(2,1)} %collective-permute-done.15.refs_4_), channel_id=1, source_target_pairs={{0,4},{4,0},{8,12},{12,8},{16,20},{20,16},{24,28},{28,24},{1,5},{5... | collective-permute-start | bytes 1474568 | tf_op jit(solution)/shard_map/ppermute | solution.py:21
  100.1 22.8 %collective-permute-start.18 = (bf16[80,3072]{1,0:T(8,128)(2,1)}, bf16[80,3072]{1,0:T(8,128)(2,1)}, u32[]{:S(2)}, u32[]{:S(2)}) collective-permute-start(bf16[80,3072]{1,0:T(8,128)(2,1)} %collective-permute-done.14.refs_2_), channel_id=1, source_target_pairs={{0,4},{4,0},{8,12},{12,8},{16,20},{20,16},{24,28},{28,24},{1,5},{5... | collective-permute-start | bytes 1474568 | tf_op jit(solution)/shard_map/ppermute | solution.py:21
  126.9 27.2 %collective-permute-start.23 = (bf16[80,3072]{1,0:T(8,128)(2,1)}, bf16[80,3072]{1,0:T(8,128)(2,1)S(1)}, u32[]{:S(2)}, u32[]{:S(2)}) collective-permute-start(bf16[80,3072]{1,0:T(8,128)(2,1)} %collective-permute-done.22.refs_6_), channel_id=1, source_target_pairs={{0,4},{4,0},{8,12},{12,8},{16,20},{20,16},{24,28},{28,24},{1,5},{5... | collective-permute-start | bytes 1474568 | tf_op jit(solution)/shard_map/ppermute | solution.py:21
  149.6 53.6 %collective-permute-start.21 = (bf16[320,1024]{1,0:T(8,128)(2,1)}, bf16[320,1024]{1,0:T(8,128)(2,1)}, u32[]{:S(2)}, u32[]{:S(2)}) collective-permute-start(bf16[320,1024]{1,0:T(8,128)(2,1)} %slice.187), channel_id=1, source_target_pairs={{0,4},{4,0},{8,12},{12,8},{16,20},{20,16},{24,28},{28,24},{1,5},{5... | collective-permute-start | bytes 1966088 | tf_op jit(solution)/shard_map/ppermute | solution.py:21
  162.0 41.1 %collective-permute-start.30 = (bf16[320,1024]{1,0:T(8,128)(2,1)}, bf16[320,1024]{1,0:T(8,128)(2,1)}, u32[]{:S(2)}, u32[]{:S(2)}) collective-permute-start(bf16[320,1024]{1,0:T(8,128)(2,1)} %slice.186), channel_id=1, source_target_pairs={{0,4},{4,0},{8,12},{12,8},{16,20},{20,16},{24,28},{28,24},{1,5},{5... | collective-permute-start | bytes 1966088 | tf_op jit(solution)/shard_map/ppermute | solution.py:21
  169.5 39.6 %collective-permute-start.33 = (bf16[320,1024]{1,0:T(8,128)(2,1)S(1)}, bf16[320,1024]{1,0:T(8,128)(2,1)}, u32[]{:S(2)}, u32[]{:S(2)}) collective-permute-start(bf16[320,1024]{1,0:T(8,128)(2,1)S(1)} %slice.185), channel_id=1, source_target_pairs={{0,4},{4,0},{8,12},{12,8},{16,20},{20,16},{24,28},{28,24},{1,5},{5... | collective-permute-start | bytes 1966088 | tf_op jit(solution)/shard_map/ppermute | solution.py:21
  207.0 21.9 %collective-permute-start.31 = (bf16[160,1024]{1,0:T(8,128)(2,1)S(1)}, bf16[160,1024]{1,0:T(8,128)(2,1)S(1)}, u32[]{:S(2)}, u32[]{:S(2)}) collective-permute-start(bf16[160,1024]{1,0:T(8,128)(2,1)S(1)} %slice.189), channel_id=1, source_target_pairs={{0,8},{4,12},{8,0},{12,4},{16,24},{20,28},{24,16},{28,20},{1,9},{5... | collective-permute-start | bytes 983048 | tf_op jit(solution)/shard_map/ppermute | solution.py:21
  207.6 24.1 %collective-permute-start.28 = (bf16[160,1024]{1,0:T(8,128)(2,1)S(1)}, bf16[160,1024]{1,0:T(8,128)(2,1)S(1)}, u32[]{:S(2)}, u32[]{:S(2)}) collective-permute-start(bf16[160,1024]{1,0:T(8,128)(2,1)S(1)} %slice.190), channel_id=1, source_target_pairs={{0,8},{4,12},{8,0},{12,4},{16,24},{20,28},{24,16},{28,20},{1,9},{5... | collective-permute-start | bytes 983048 | tf_op jit(solution)/shard_map/ppermute | solution.py:21
  210.4 21.8 %collective-permute-start.34 = (bf16[160,1024]{1,0:T(8,128)(2,1)S(1)}, bf16[160,1024]{1,0:T(8,128)(2,1)S(1)}, u32[]{:S(2)}, u32[]{:S(2)}) collective-permute-start(bf16[160,1024]{1,0:T(8,128)(2,1)S(1)} %slice.188), channel_id=1, source_target_pairs={{0,8},{4,12},{8,0},{12,4},{16,24},{20,28},{24,16},{28,20},{1,9},{5... | collective-permute-start | bytes 983048 | tf_op jit(solution)/shard_map/ppermute | solution.py:21
  229.0 23.9 %collective-permute-start.32 = (bf16[80,1024]{1,0:T(8,128)(2,1)S(1)}, bf16[80,1024]{1,0:T(8,128)(2,1)S(1)}, u32[]{:S(2)}, u32[]{:S(2)}) collective-permute-start(bf16[80,1024]{1,0:T(8,128)(2,1)S(1)} %slice.192), channel_id=1, source_target_pairs={{0,16},{4,20},{8,24},{12,28},{16,0},{20,4},{24,8},{28,12},{1,17},{... | collective-permute-start | bytes 491528 | tf_op jit(solution)/shard_map/ppermute | solution.py:21
  231.8 21.1 %collective-permute-start.29 = (bf16[80,1024]{1,0:T(8,128)(2,1)S(1)}, bf16[80,1024]{1,0:T(8,128)(2,1)S(1)}, u32[]{:S(2)}, u32[]{:S(2)}) collective-permute-start(bf16[80,1024]{1,0:T(8,128)(2,1)S(1)} %slice.193), channel_id=1, source_target_pairs={{0,16},{4,20},{8,24},{12,28},{16,0},{20,4},{24,8},{28,12},{1,17},{... | collective-permute-start | bytes 491528 | tf_op jit(solution)/shard_map/ppermute | solution.py:21
  232.3 20.7 %collective-permute-start.35 = (bf16[80,1024]{1,0:T(8,128)(2,1)S(1)}, bf16[80,1024]{1,0:T(8,128)(2,1)S(1)}, u32[]{:S(2)}, u32[]{:S(2)}) collective-permute-start(bf16[80,1024]{1,0:T(8,128)(2,1)S(1)} %slice.191), channel_id=1, source_target_pairs={{0,16},{4,20},{8,24},{12,28},{16,0},{20,4},{24,8},{28,12},{1,17},{... | collective-permute-start | bytes 491528 | tf_op jit(solution)/shard_map/ppermute | solution.py:21
  (36 other events, 279.2 us)
